TPU v7x, 768 devices: a whole 4x8x12 slice. The times are simulated.
768 devices in a mesh: dp: 4 (over x), seq: 96 (over z, y), tensor: 2 (over core).
Axes of the slice: x: 4, y: 8, z: 12, core: 2. Of those that a mesh axis runs over, the one named last changes fastest.
Arguments:
- hidden: bfloat16 [4, 49152, 4096], P('dp', ('seq', 'tensor')), may hold values from -6 to 6
- lengths: int32 [4, 12], replicated, may hold values from 1 to 12288, 49152 in all within a row
- positive: int32 [48], replicated, may hold values from 0 to 47, as said below
- gain: float32 [4096], replicated, may hold values from 0.5 to 1.5
Outputs:
- hidden_grad: bfloat16 [4, 49152, 4096], P('dp', ('seq', 'tensor'))
- loss: float32 [], replicated
Inputs may be any that keep to these rules, and one draw needn't show every extreme that they name: Each sequence's 12 lengths sum to 49152. positive[i] != i and positive[positive[i]] = i.
All inputs are finite; a program needn't handle non-finite values.
Results may differ from a plain program's by a relative error of at most 0.002.
Values sent between devices are 32-bit elements; how exact they have to be, the bound alone decides.
No kernel may reach another device: no remote copies, remote signals or barrier semaphores. Data moves between devices by JAX's collectives and lax.ppermute only.
A program may use at most 32 MiB of HBM per device.

v0:
```python
import jax
import jax.numpy as jnp
from jax import lax
from jax.sharding import PartitionSpec as P

tau_value = 0.05
loss_factor = 65536.0
norm_eps = 1e-06
embed_eps = 1e-12


def membership(lens, positions):
    ends = jnp.cumsum(lens)
    starts = ends - lens
    inside = (positions[None, :] >= starts[:, None]) & (positions[None, :] < ends[:, None])
    return inside.astype(jnp.float32)


def contrast(means, positive):
    square = jnp.sum(means * means, axis=1)
    inverse = 1.0 / jnp.sqrt(square + embed_eps)
    unit = means * inverse[:, None]
    scores = jnp.dot(unit, unit.T, precision=lax.Precision.HIGHEST) / tau_value
    count = means.shape[0]
    ident = lax.iota(jnp.int32, count)
    offdiag = (ident[:, None] != ident[None, :]).astype(jnp.float32)
    weights = jnp.exp(scores) * offdiag
    totals = jnp.sum(weights, axis=1)
    picked = (ident[None, :] == positive[:, None]).astype(jnp.float32)
    loss = jnp.sum(jnp.log(totals) - jnp.sum(scores * picked, axis=1))
    grad_scores = weights / totals[:, None] - picked
    grad_unit = (
        jnp.dot(grad_scores + grad_scores.T, unit, precision=lax.Precision.HIGHEST) / tau_value
    )
    along = jnp.sum(means * grad_unit, axis=1)
    grad_means = grad_unit * inverse[:, None] - means * (inverse**3 * along)[:, None]
    return (loss, grad_means)


def shards(hidden, lengths, positive, gain):
    rows = hidden[0]
    tok = rows.shape[0]
    width = rows.shape[1]
    docs = lengths.shape[1]
    group = lax.axis_index("dp")
    shard = lax.axis_index(("seq", "tensor"))
    lens = lax.dynamic_index_in_dim(lengths, group, 0, keepdims=False)
    values = rows.astype(jnp.float32)
    scale = lax.rsqrt(jnp.mean(values * values, axis=1) + norm_eps)
    positions = shard * tok + lax.iota(jnp.int32, tok)
    member = membership(lens, positions)
    contrib = jnp.dot(member * scale[None, :], values, precision=lax.Precision.HIGHEST)
    sums = lax.psum(contrib, ("seq", "tensor"))
    own_means = sums * gain[None, :] / lens.astype(jnp.float32)[:, None]
    means = lax.all_gather(own_means, "dp", axis=0, tiled=True)
    loss, grad_means = contrast(means, positive)
    own_grads = lax.dynamic_slice_in_dim(grad_means, group * docs, docs, 0)
    per_doc = own_grads / lens.astype(jnp.float32)[:, None]
    grad_y = jnp.dot(member.T, per_doc, precision=lax.Precision.HIGHEST)
    weighted = grad_y * gain[None, :]
    inner = jnp.sum(weighted * values, axis=1)
    grad_rows = loss_factor * (
        weighted * scale[:, None] - values * (scale**3 * inner / width)[:, None]
    )
    return (grad_rows.astype(jnp.bfloat16)[None], loss)


def solution(mesh):
    return jax.shard_map(
        shards,
        mesh=mesh,
        in_specs=(P("dp", ("seq", "tensor"), None), P(), P(), P()),
        out_specs=(P("dp", ("seq", "tensor"), None), P()),
        check_vma=False,
    )
```

profile of v0, /device:TPU:1, one launch (start us, length us, event | category | flops | bytes accessed | tf_op | source)
XLA Modules:
  0.0 340.7 jit_solution(10352800097478325068)
XLA Ops:
  7.2 0.0 copy-start.1
  7.2 0.0 all-reduce.2.cloned.1.call-start
  7.2 2.1 fusion
  9.3 0.7 bitcast_convert_fusion
  10.0 0.2 reduce-window.7
  10.2 0.7 bitcast_subtract_fusion
  10.9 3.3 fusion.6
  14.2 0.0 all-reduce.2.cloned.1.call-update
  14.2 295.1 %all-reduce.2.cloned.1.call-done = f32[12,4096]{1,0:T(8,128)} async-done(((f32[12,4096]{1,0:T(8,128)}), f32[12,4096]{1,0:T(8,128)}) %all-reduce.2.cloned.1.call-update) | async-done | bytes 196624 | tf_op jit(solution)/shard_map/psum | solution.py:53
  309.3 0.0 copy-done.1
  309.3 1.0 divide_bitcast_fusion
  310.3 14.1 %all-gather = f32[4,12,4096]{2,1,0:T(8,128)} all-gather(f32[1,12,4096]{2,1,0:T(8,128)S(1)} %divide_bitcast_fusion), channel_id=1, replica_groups=mesh['dp'=4,'seq'=96,'tensor'=2] {'dp'}, dimensions={0}, use_global_device_ids=true | all-gather | bytes 983040 | tf_op jit(solution)/shard_map/all_gather | solution.py:55
  324.5 1.3 reshape.76
  325.8 0.2 multiply_reduce_fusion.1
  326.0 0.9 convolution_multiply_fusion.1
  326.9 0.0 copy-done.2
  326.9 0.1 copy.8
  327.0 0.6 subtract_reduce_fusion
  327.6 1.1 multiply_reduce_fusion
  328.7 0.1 dynamic-slice
  328.8 0.1 dynamic-slice.1
  328.8 0.0 copy-done
  328.8 2.4 fusion.1
  331.3 2.5 fusion.5
  (8 shorter events, 0.1 us)
Async XLA Ops:
  7.2 302.1 %copy-start.1 = (f32[4096]{0:T(1024)S(1)}, f32[4096]{0:T(1024)}, u32[]{:S(2)}) copy-start(f32[4096]{0:T(1024)} %param.7) | copy-start | bytes 49156
  7.2 302.1 %all-reduce.2.cloned.1.call-start = ((), (), s32[]{:S(2)}) async-start(), calls=%async_computation | async-start | bytes 524288 | tf_op jit(solution)/shard_map/psum | solution.py:53
  9.3 317.6 %copy-start.2 = (s32[48]{0:T(128)S(1)}, s32[48]{0:T(128)}, u32[]{:S(2)}) copy-start(s32[48]{0:T(128)} %param.6) | copy-start | bytes 580
  14.2 314.6 %copy-start = (bf16[1,256,4096]{2,1,0:T(8,128)(2,1)S(1)}, bf16[1,256,4096]{2,1,0:T(8,128)(2,1)}, u32[]{:S(2)}) copy-start(bf16[1,256,4096]{2,1,0:T(8,128)(2,1)} %param.4) | copy-start | bytes 6291460
Sparse Core Ops, SparseCore 0:
  14.3 294.9 all-reduce.1
where the time goes:
time: 343 us; the launch traced here: 341 us
  waiting for transfers between devices  295 us (86%)
  blocking collectives  14.1 us (4%)
  between operations  14.1 us (4%)
  other arithmetic  8.08 us (2%)
  matrix products  7.66 us (2%)
    psum x1, waiting for transfers between devices, shards(): sums = lax.psum(contrib, ('seq', 'tensor'))  295 us
    all_gather x1, blocking collectives, shards(): means = lax.all_gather(own_means, 'dp', axis=0, tiled=True)  14.1 us
  transfers between devices with their start and end apart: 1, of which 1 were waited for; matrix products, arithmetic and copies ran while one was open for 0% of the time, Pallas kernels for 0%

commit v1 on v0

v1 whole, which is shorter than its diff:
```python
import functools

import jax
import jax.numpy as jnp
from jax import lax
from jax.experimental import pallas as pl
from jax.experimental.pallas import tpu as pltpu
from jax.sharding import Mesh
from jax.sharding import PartitionSpec as P

tau_value = 0.05
loss_factor = 65536.0
norm_eps = 1e-06
embed_eps = 1e-12

LANES = 128
DOC_ROWS = 16
HIGHEST = lax.Precision.HIGHEST


def doc_bounds(lens_ref, group, docs, shape):
    doc = lax.broadcasted_iota(jnp.int32, shape, 1) % DOC_ROWS
    starts = jnp.zeros(shape, jnp.int32)
    ends = jnp.zeros(shape, jnp.int32)
    total = jnp.int32(0)
    for d in range(docs):
        size = lens_ref[group, d]
        starts = jnp.where(doc == d, total, starts)
        total = total + size
        ends = jnp.where(doc == d, total, ends)
    return starts, ends


def one_hot(lens_ref, group, first, docs, tok):
    starts, ends = doc_bounds(lens_ref, group, docs, (1, LANES))
    positions = first + lax.broadcasted_iota(jnp.int32, (tok, LANES), 0)
    inside = (positions >= starts) & (positions < ends)
    return jnp.where(inside, 1.0, 0.0)


def halves(x):
    high = x.astype(jnp.bfloat16)
    low = (x - high.astype(jnp.float32)).astype(jnp.bfloat16)
    return high, low


def row_scale(values):
    width = values.shape[1]
    return lax.rsqrt(jnp.sum(values * values, axis=1, keepdims=True) * (1.0 / width) + norm_eps)


def shard_number(sizes):
    _, _, n_y, n_t = sizes
    return (lax.axis_index("z") * n_y + lax.axis_index("y")) * n_t + lax.axis_index("t")


def pool_kernel(sizes, lens_ref, rows_ref, out_ref):
    docs = lens_ref.shape[1]
    tok, width = rows_ref.shape
    blocks = out_ref.shape[0]
    columns = width // blocks // LANES
    scale = row_scale(rows_ref[...].astype(jnp.float32))
    member = one_hot(lens_ref, lax.axis_index("dp"), shard_number(sizes) * tok, docs, tok)
    high, low = halves(member * scale)
    lane = lax.broadcasted_iota(jnp.int32, (tok, LANES), 1)
    weights = jnp.where(lane < DOC_ROWS, high.astype(jnp.float32), low.astype(jnp.float32))
    weights = weights.astype(jnp.bfloat16)
    for block in range(blocks):
        cut = width // blocks
        part = lax.dot_general(
            weights, rows_ref[:, block * cut : (block + 1) * cut],
            (((0,), (0,)), ((), ())), preferred_element_type=jnp.float32,
        )
        both = part[:docs] + part[DOC_ROWS : DOC_ROWS + docs]
        for column in range(columns):
            out_ref[block, column * docs : (column + 1) * docs, :] = both[
                :, column * LANES : (column + 1) * LANES
            ]


def sum_kernel(parts_ref, out_ref):
    total = parts_ref[0]
    for k in range(1, parts_ref.shape[0]):
        total = total + parts_ref[k]
    for k in range(out_ref.shape[0]):
        out_ref[k] = total


def contrast(means, lens_ref, positive_ref, group, docs):
    count = means.shape[0]
    gram = lax.dot_general(
        means, means, (((1,), (1,)), ((), ())), precision=HIGHEST, preferred_element_type=jnp.float32
    )
    row = lax.broadcasted_iota(jnp.int32, (count, count), 0)
    col = lax.broadcasted_iota(jnp.int32, (count, count), 1)
    diagonal = jnp.where(row == col, gram, 0.0)
    inv_col = 1.0 / jnp.sqrt(jnp.sum(diagonal, axis=1, keepdims=True) + embed_eps)
    inv_row = 1.0 / jnp.sqrt(jnp.sum(diagonal, axis=0, keepdims=True) + embed_eps)
    scores = gram * inv_col * inv_row * (1.0 / tau_value)
    weights = jnp.where(row == col, 0.0, jnp.exp(scores))
    totals_col = jnp.sum(weights, axis=1, keepdims=True)
    totals_row = jnp.sum(weights, axis=0, keepdims=True)
    picked = jnp.where(positive_ref[...] == row, 1.0, 0.0)
    loss = jnp.sum(jnp.log(totals_row), axis=1, keepdims=True) - jnp.sum(
        jnp.sum(scores * picked, axis=0, keepdims=True), axis=1, keepdims=True
    )
    both = weights / totals_col + weights / totals_row - 2.0 * picked
    along = jnp.sum(both * scores, axis=1, keepdims=True)
    mix = both * (inv_col * inv_row * (1.0 / tau_value))
    mix = mix - jnp.where(row == col, inv_col * inv_col * along, 0.0)
    doc = lax.broadcasted_iota(jnp.int32, (DOC_ROWS, count), 0)
    other = lax.broadcasted_iota(jnp.int32, (DOC_ROWS, count), 1)
    own = jnp.where((other == doc + group * docs) & (doc < docs), 1.0, 0.0)
    size = jnp.ones((DOC_ROWS, 1), jnp.float32)
    at = lax.broadcasted_iota(jnp.int32, (DOC_ROWS, 1), 0)
    for d in range(docs):
        size = jnp.where(at == d, lens_ref[group, d].astype(jnp.float32), size)
    own_mix = jnp.dot(own, mix, precision=HIGHEST, preferred_element_type=jnp.float32)
    return loss, own_mix * (loss_factor / size)


def grad_kernel(sizes, lens_ref, positive_ref, gain_ref, sums_ref, rows_ref, out_ref, loss_ref, means_ref, grads_ref):
    n_dp, _, n_y, n_t = sizes
    docs = lens_ref.shape[1]
    tok, width = rows_ref.shape
    group = lax.axis_index("dp")
    step = pl.program_id(0)
    columns = width // (n_y * n_t) // LANES

    @pl.when(step == 0)
    def _():
        for t in range(n_t):
            for g in range(n_dp):
                for y in range(n_y):
                    for column in range(columns):
                        start = ((y * n_t + t) * columns + column) * LANES
                        means_ref[g * docs : (g + 1) * docs, start : start + LANES] = sums_ref[
                            t, g * n_y + y, column * docs : (column + 1) * docs, :
                        ]
        at = lax.broadcasted_iota(jnp.int32, (n_dp * docs, 1), 0)
        size = jnp.ones((n_dp * docs, 1), jnp.float32)
        for g in range(n_dp):
            for d in range(docs):
                size = jnp.where(at == g * docs + d, lens_ref[g, d].astype(jnp.float32), size)
        means = means_ref[...] * gain_ref[...] * (1.0 / size)
        loss, mix = contrast(means, lens_ref, positive_ref, group, docs)
        loss_ref[...] = loss
        grads = jnp.dot(mix, means, precision=HIGHEST, preferred_element_type=jnp.float32)
        high, low = halves(grads * gain_ref[...])
        grads_ref[:DOC_ROWS] = high
        grads_ref[DOC_ROWS:] = low

    values = rows_ref[...].astype(jnp.float32)
    scale = row_scale(values)
    first = (shard_number(sizes) * pl.num_programs(0) + step) * tok
    member = one_hot(lens_ref, group, first, docs, tok)[:, : 2 * DOC_ROWS].astype(jnp.bfloat16)
    weighted = jnp.dot(member, grads_ref[...], preferred_element_type=jnp.float32)
    inner = jnp.sum(weighted * values, axis=1, keepdims=True)
    out = weighted * scale - values * (scale * scale * scale * inner * (1.0 / width))
    out_ref[...] = out.astype(jnp.bfloat16)


def shards(sizes, hidden, lengths, positive, gain):
    n_dp, n_z, n_y, n_t = sizes
    rows = hidden[0]
    tok, width = rows.shape
    docs = lengths.shape[1]
    blocks = n_y * n_t
    lines = docs * width // blocks // LANES
    smem = pl.BlockSpec(memory_space=pltpu.SMEM)
    vmem = pl.BlockSpec(memory_space=pltpu.VMEM)
    params = pltpu.CompilerParams(vmem_limit_bytes=40 * 2**20)

    def summed(parts, copies):
        return pl.pallas_call(
            sum_kernel,
            out_shape=jax.ShapeDtypeStruct((copies, lines, LANES), jnp.float32),
            in_specs=[vmem], out_specs=vmem, compiler_params=params,
        )(parts)

    share = pl.pallas_call(
        functools.partial(pool_kernel, sizes),
        out_shape=jax.ShapeDtypeStruct((blocks, lines, LANES), jnp.float32),
        in_specs=[smem, vmem], out_specs=vmem, compiler_params=params,
    )(lengths, rows)
    parts = lax.all_to_all(share, ("y", "t"), 0, 0, tiled=True)
    parts = lax.all_to_all(summed(parts, n_z), "z", 0, 0, tiled=True)
    parts = lax.all_to_all(summed(parts, n_dp * n_y), ("dp", "y"), 0, 0, tiled=True)
    sums = lax.all_gather(parts, "t", axis=0)

    steps = 4
    whole = lambda *dims: pl.BlockSpec(dims, lambda i: (0,) * len(dims))
    grads, loss = pl.pallas_call(
        functools.partial(grad_kernel, sizes),
        grid=(steps,),
        out_shape=(
            jax.ShapeDtypeStruct((tok, width), jnp.bfloat16),
            jax.ShapeDtypeStruct((1, 1), jnp.float32),
        ),
        in_specs=[
            smem,
            whole(1, n_dp * docs),
            whole(1, width),
            whole(*sums.shape),
            pl.BlockSpec((tok // steps, width), lambda i: (i, 0)),
        ],
        out_specs=(pl.BlockSpec((tok // steps, width), lambda i: (i, 0)), whole(1, 1)),
        scratch_shapes=[
            pltpu.VMEM((n_dp * docs, width), jnp.float32),
            pltpu.VMEM((2 * DOC_ROWS, width), jnp.bfloat16),
        ],
        compiler_params=params,
    )(lengths, positive.reshape(1, -1), gain.reshape(1, -1), sums, rows)
    return grads[None], loss.reshape(())


def solution(mesh):
    n_dp, n_seq, n_t = mesh.devices.shape
    n_y = 8 if n_seq % 8 == 0 else 2
    sizes = (n_dp, n_seq // n_y, n_y, n_t)
    inner = Mesh(mesh.devices.reshape(sizes), ("dp", "z", "y", "t"))
    split = P("dp", ("z", "y", "t"), None)
    return jax.shard_map(
        functools.partial(shards, sizes),
        mesh=inner,
        in_specs=(split, P(), P(), P()),
        out_specs=(split, P()),
        check_vma=False,
    )
```

time: 343 us -> 78.6 us (0.23)
  waiting for transfers between devices: 295 us -> 0 us
  blocking collectives: 14.1 us -> 67.2 us
  between operations: 14.1 us -> 0.69 us
  other arithmetic: 8.08 us -> 0 us
  Pallas kernels: 0 us -> 8.04 us
  matrix products: 7.66 us -> 0 us
    psum x1 -> x0, waiting for transfers between devices: 295 us -> none  [shards(): sums = lax.psum(contrib, ('seq', 'tensor'))]
    all_to_all x0 -> x3, blocking collectives: none -> 60 us  [the longest x1 23.4 us: shards(): parts = lax.all_to_all(share, ('y', 't'), 0, 0, tiled=True)]
    pallas_call x0 -> x4, Pallas kernels: none -> 8.04 us  [the longest x1 6.41 us: shards(): pl.pallas_call(functools.partial(grad_kernel, sizes), grid=(steps,), out_...]
    dot_general x4 -> x0, matrix products: 7.66 us -> none  [the longest x1 3.27 us: shards(): jnp.dot(member * scale[None, :], values, precision=lax.Precision.HIGHEST)]
    all_gather x1, blocking collectives: 14.1 us -> 7.24 us  [shards(): sums = lax.all_gather(parts, 't', axis=0)]
  transfers between devices with their start and end apart: 1 -> 0, of which waited for: 1 -> 0; matrix products, arithmetic and copies ran while one was open for 0% -> 0% of each run, Pallas kernels for 0% -> 0%
where the time goes in v1:
time: 78.6 us; the launch traced here: 78.2 us
  blocking collectives  67.2 us (85%)
  Pallas kernels  8.04 us (10%)
  local copies, waits for them, and re-layouts  2.29 us (3%)
    all_to_all x1, blocking collectives, shards(): parts = lax.all_to_all(share, ('y', 't'), 0, 0, tiled=True)  23.4 us
    all_to_all x1, blocking collectives, shards(): parts = lax.all_to_all(summed(parts, n_z), 'z', 0, 0, tiled=True)  21.9 us
    all_to_all x1, blocking collectives, shards(): lax.all_to_all(summed(parts, n_dp * n_y), ('dp', 'y'), 0, 0, tiled=True)  14.6 us
    all_gather x1, blocking collectives, shards(): sums = lax.all_gather(parts, 't', axis=0)  7.24 us
    pallas_call x1, Pallas kernels, shards(): pl.pallas_call(functools.partial(grad_kernel, sizes), grid=(steps,), out_...  6.41 us
    unnamed x12, local copies, waits for them, and re-layouts  2.29 us

profile of v1, /device:TPU:1, one launch (start us, length us, event | category | flops | bytes accessed | tf_op | source)
XLA Modules:
  0.0 78.2 jit_solution(8207531950406249225)
XLA Ops:
  0.6 0.0 copy-start
  0.6 1.6 %copy-done = bf16[1,256,4096]{2,1,0:T(8,128)(2,1)S(1)} copy-done((bf16[1,256,4096]{2,1,0:T(8,128)(2,1)S(1)}, bf16[1,256,4096]{2,1,0:T(8,128)(2,1)}, u32[]{:S(2)}) %copy-start) | copy-done | bytes 2097176
  2.2 0.0 copy-start.3
  2.2 0.7 copy-done.3
  2.9 1.6 %shard_map.59 = f32[16,24,128]{2,1,0:T(8,128)S(1)} custom-call(s32[4,12]{1,0:T(4,128)S(1)} %copy-done.3, bf16[256,4096]{1,0:T(8,128)(2,1)S(1)} %bitcast.6), custom_call_target="tpu_custom_call" | custom-call | tf_op jit(solution)/shard_map/pallas_call | solution.py:181
  4.5 0.0 copy-start.1
  4.5 0.0 copy-start.2
  4.5 0.0 copy-start.4
  4.5 0.0 copy-start.5
  4.5 23.4 %all_to_all.15.parts_ref = f32[16,24,128]{2,1,0:T(8,128)S(1)} all-to-all(f32[16,24,128]{2,1,0:T(8,128)S(1)} %shard_map.59), channel_id=1, replica_groups=mesh['dp'=4,'z'=12,'y'=8,'t'=2] {'y','t'}, dimensions={0} | all-to-all | bytes 393216 | tf_op jit(solution)/shard_map/all_to_all | solution.py:186
  28.0 21.9 %all_to_all.16.parts_ref = f32[12,24,128]{2,1,0:T(8,128)S(1)} all-to-all(f32[12,24,128]{2,1,0:T(8,128)S(1)} %shard_map.60), channel_id=1, replica_groups=mesh['dp'=4,'z'=12,'y'=8,'t'=2] {'z'}, dimensions={0} | all-to-all | bytes 294912 | tf_op jit(solution)/shard_map/all_to_all | solution.py:187
  49.9 14.6 %all_to_all.17 = f32[32,24,128]{2,1,0:T(8,128)S(1)} all-to-all(f32[32,24,128]{2,1,0:T(8,128)S(1)} %shard_map.61), channel_id=1, replica_groups=mesh['dp'=4,'z'=12,'y'=8,'t'=2] {'dp','y'}, dimensions={0} | all-to-all | bytes 786432 | tf_op jit(solution)/shard_map/all_to_all | solution.py:188
  64.6 7.2 %all-gather = f32[64,24,128]{2,1,0:T(8,128)S(1)} all-gather(f32[32,24,128]{2,1,0:T(8,128)S(1)} %all_to_all.17), channel_id=2, replica_groups=mesh['dp'=4,'z'=12,'y'=8,'t'=2] {'t'}, dimensions={0}, use_global_device_ids=true | all-gather | bytes 1179648 | tf_op jit(solution)/shard_map/all_gather | solution.py:189
  71.8 0.0 copy-done.1
  71.8 0.0 copy-done.2
  71.8 0.0 copy-done.4
  71.8 0.0 copy-done.5
  71.8 6.4 %shard_map.62 = (bf16[256,4096]{1,0:T(8,128)(2,1)}, f32[1,1]{1,0:T(1,128)}) custom-call(s32[4,12]{1,0:T(4,128)S(1)} %copy-done.4, s32[1,48]{1,0:T(1,128)S(1)} %bitcast.10, f32[1,4096]{1,0:T(1,128)S(1)} %bitcast.9, f32[2,32,24,128]{3,2,1,0:T(8,128)S(1)} %bitcast.8, bf16[256,4096]{1,0:T(8,128)(2,1)S(1)} %bitcast.7), custom_call_target="tpu_custom_call" | custom-call | tf_op jit(solution)/shard_map/pallas_call | solution.py:193
  (2 shorter events, 0.1 us)
Async XLA Ops:
  0.6 1.6 %copy-start = (bf16[1,256,4096]{2,1,0:T(8,128)(2,1)S(1)}, bf16[1,256,4096]{2,1,0:T(8,128)(2,1)}, u32[]{:S(2)}) copy-start(bf16[1,256,4096]{2,1,0:T(8,128)(2,1)} %param.4) | copy-start | bytes 6291460
  2.2 0.7 copy-start.3
  4.5 67.3 %copy-start.1 = (bf16[1,256,4096]{2,1,0:T(8,128)(2,1)S(1)}, bf16[1,256,4096]{2,1,0:T(8,128)(2,1)}, u32[]{:S(2)}) copy-start(bf16[1,256,4096]{2,1,0:T(8,128)(2,1)} %param.4) | copy-start | bytes 6291460
  4.5 67.3 %copy-start.2 = (f32[4096]{0:T(1024)S(1)}, f32[4096]{0:T(1024)}, u32[]{:S(2)}) copy-start(f32[4096]{0:T(1024)} %param.7) | copy-start | bytes 49156
  4.5 67.3 %copy-start.4 = (s32[4,12]{1,0:T(4,128)S(1)}, s32[4,12]{1,0:T(4,128)}, u32[]{:S(2)}) copy-start(s32[4,12]{1,0:T(4,128)} %lens_ref.3) | copy-start | bytes 580
  4.5 67.3 %copy-start.5 = (s32[48]{0:T(128)S(1)}, s32[48]{0:T(128)}, u32[]{:S(2)}) copy-start(s32[48]{0:T(128)} %param.6) | copy-start | bytes 580

commit v2 on v1

v2 whole, which is shorter than its diff:
```python
import functools

import jax
import jax.numpy as jnp
from jax import lax
from jax.experimental import pallas as pl
from jax.experimental.pallas import tpu as pltpu
from jax.sharding import Mesh
from jax.sharding import PartitionSpec as P

tau_value = 0.05
loss_factor = 65536.0
norm_eps = 1e-06
embed_eps = 1e-12

LANES = 128
DOC_ROWS = 16
CHUNKS = 8
STEPS = 4
Z_ORDER = tuple(range(11, -1, -1))
HIGHEST = lax.Precision.HIGHEST


def one_hot(lens_ref, group, first, docs, tok):
    doc = lax.broadcasted_iota(jnp.int32, (1, LANES), 1) % DOC_ROWS
    starts = jnp.zeros((1, LANES), jnp.int32)
    ends = jnp.zeros((1, LANES), jnp.int32)
    total = jnp.int32(0)
    for d in range(docs):
        size = lens_ref[group, d]
        starts = jnp.where(doc == d, total, starts)
        total = total + size
        ends = jnp.where(doc == d, total, ends)
    positions = first + lax.broadcasted_iota(jnp.int32, (tok, LANES), 0)
    return jnp.where((positions >= starts) & (positions < ends), 1.0, 0.0)


def halves(x):
    high = x.astype(jnp.bfloat16)
    return high, (x - high.astype(jnp.float32)).astype(jnp.bfloat16)


def thirds(x):
    high = x.astype(jnp.bfloat16)
    rest = x - high.astype(jnp.float32)
    return (high,) + halves(rest)


def pool_kernel(
    sizes, lens_hbm, rows_hbm, out_ref, member_ref, scale_ref, inverse_ref, lens_ref, rows_ref, weights_ref, sems
):
    n_dp, _, n_y, n_t = sizes
    docs = lens_ref.shape[1]
    tok, width = rows_ref.shape
    blocks = out_ref.shape[0]
    cut = width // blocks
    lens_copy = pltpu.make_async_copy(lens_hbm, lens_ref, sems.at[CHUNKS])
    lens_copy.start()
    copies = []
    for chunk in range(CHUNKS):
        at = pl.ds(chunk * (tok // CHUNKS), tok // CHUNKS)
        copies.append(pltpu.make_async_copy(rows_hbm.at[at], rows_ref.at[at], sems.at[chunk]))
        copies[-1].start()
    lens_copy.wait()
    shard = (lax.axis_index("z") * n_y + lax.axis_index("y")) * n_t + lax.axis_index("t")
    member_ref[...] = one_hot(lens_ref, lax.axis_index("dp"), shard * tok, docs, tok)
    line = lax.broadcasted_iota(jnp.int32, inverse_ref.shape, 0)
    size = jnp.ones(inverse_ref.shape, jnp.float32)
    for g in range(n_dp):
        for d in range(docs):
            size = jnp.where(line == g * docs + d, lens_ref[g, d].astype(jnp.float32), size)
    inverse_ref[...] = 1.0 / size
    for chunk in range(CHUNKS):
        at = pl.ds(chunk * (tok // CHUNKS), tok // CHUNKS)
        copies[chunk].wait()
        values = rows_ref[at].astype(jnp.float32)
        scale = lax.rsqrt(jnp.sum(values * values, axis=1, keepdims=True) * (1.0 / width) + norm_eps)
        scale_ref[at] = jnp.broadcast_to(scale, (tok // CHUNKS, LANES))
        weights_ref[at] = member_ref[at] * scale
    high, low = halves(jnp.transpose(weights_ref[...])[:DOC_ROWS])
    weights = jnp.concatenate([high, low], axis=0)
    for block in range(blocks):
        part = jnp.dot(
            weights, rows_ref[:, block * cut : (block + 1) * cut], preferred_element_type=jnp.float32
        )
        both = part[:docs] + part[DOC_ROWS : DOC_ROWS + docs]
        for column in range(cut // LANES):
            out_ref[block, column * docs : (column + 1) * docs, :] = both[
                :, column * LANES : (column + 1) * LANES
            ]


def sum_kernel(parts_ref, out_ref):
    total = parts_ref[0]
    for k in range(1, parts_ref.shape[0]):
        total = total + parts_ref[k]
    for k in range(out_ref.shape[0]):
        out_ref[k] = total


def contrast(parts, positive_ref, inverse, group, docs):
    count = parts.shape[0] // 3
    cross = lax.dot_general(parts, parts, (((1,), (1,)), ((), ())), preferred_element_type=jnp.float32)
    cross = cross[:count] + cross[count : 2 * count] + cross[2 * count :]
    gram = cross[:, :count] + cross[:, count : 2 * count] + cross[:, 2 * count :]
    row = lax.broadcasted_iota(jnp.int32, (count, count), 0)
    col = lax.broadcasted_iota(jnp.int32, (count, count), 1)
    diagonal = jnp.where(row == col, gram, 0.0)
    inv_col = 1.0 / jnp.sqrt(jnp.sum(diagonal, axis=1, keepdims=True) + embed_eps)
    inv_row = 1.0 / jnp.sqrt(jnp.sum(diagonal, axis=0, keepdims=True) + embed_eps)
    pair = inv_col * inv_row * (1.0 / tau_value)
    scores = gram * pair
    weights = jnp.where(row == col, 0.0, jnp.exp(scores))
    totals_col = jnp.sum(weights, axis=1, keepdims=True)
    totals_row = jnp.sum(weights, axis=0, keepdims=True)
    picked = jnp.where(positive_ref[...] == row, 1.0, 0.0)
    loss = jnp.sum(
        jnp.log(totals_row) - jnp.sum(scores * picked, axis=0, keepdims=True), axis=1, keepdims=True
    )
    both = weights * (1.0 / totals_col + 1.0 / totals_row) - 2.0 * picked
    along = jnp.sum(both * scores, axis=1, keepdims=True)
    mix = both * pair - jnp.where(row == col, inv_col * inv_col * along, 0.0)
    mix = mix * (loss_factor * inverse[:, :1])
    doc = lax.broadcasted_iota(jnp.int32, (DOC_ROWS, count), 0)
    other = lax.broadcasted_iota(jnp.int32, (DOC_ROWS, count), 1)
    own = jnp.where((other == doc + group * docs) & (doc < docs), 1.0, 0.0)
    return loss, jnp.dot(own, mix, precision=HIGHEST, preferred_element_type=jnp.float32)


def grad_kernel(
    sizes, positive_ref, gain_ref, sums_ref, rows_ref, member_ref, scale_ref, inverse_ref,
    out_hbm, loss_ref, means_ref, parts_ref, grads_ref, weights_ref, out_ref, sems,
):
    n_dp, _, n_y, n_t = sizes
    tok, width = rows_ref.shape
    count = inverse_ref.shape[0]
    docs = count // n_dp
    columns = width // (n_y * n_t) // LANES
    for t in range(n_t):
        for g in range(n_dp):
            for y in range(n_y):
                for column in range(columns):
                    start = ((y * n_t + t) * columns + column) * LANES
                    means_ref[g * docs : (g + 1) * docs, start : start + LANES] = sums_ref[
                        t, g * n_y + y, column * docs : (column + 1) * docs, :
                    ]
    inverse = inverse_ref[...]
    means = means_ref[...] * gain_ref[...] * inverse[:, :1]
    for k, part in enumerate(thirds(means)):
        parts_ref[k * count : (k + 1) * count] = part
    loss, mix = contrast(parts_ref[...], positive_ref, inverse, lax.axis_index("dp"), docs)
    loss_ref[...] = loss
    mix = jnp.concatenate(thirds(jnp.concatenate([mix, mix, mix], axis=1)), axis=0)
    grads = jnp.dot(mix, parts_ref[...], preferred_element_type=jnp.float32)
    grads = grads[:DOC_ROWS] + grads[DOC_ROWS : 2 * DOC_ROWS] + grads[2 * DOC_ROWS :]
    high, low = halves(grads * gain_ref[...])
    grads_ref[:DOC_ROWS] = high
    grads_ref[DOC_ROWS : 2 * DOC_ROWS] = low
    grads_ref[2 * DOC_ROWS :] = high

    member, scale = member_ref[...], scale_ref[...]
    inner = lax.dot_general(
        rows_ref[...], grads_ref[: 2 * DOC_ROWS], (((1,), (1,)), ((), ())), preferred_element_type=jnp.float32
    )
    inner = jnp.sum(inner * member[:, : 2 * DOC_ROWS], axis=1, keepdims=True)
    back = scale[:, :1] * scale[:, :1] * scale[:, :1] * inner * (1.0 / width)
    high, low = halves(member * scale)
    lane = lax.broadcasted_iota(jnp.int32, member.shape, 1)
    weights = jnp.where(lane < 2 * DOC_ROWS, high.astype(jnp.float32), low.astype(jnp.float32))
    weights_ref[...] = weights.astype(jnp.bfloat16)
    copies = []
    for step in range(STEPS):
        at = slice(step * (tok // STEPS), (step + 1) * (tok // STEPS))
        forward = jnp.dot(weights_ref[at, : 3 * DOC_ROWS], grads_ref[...], preferred_element_type=jnp.float32)
        out = forward - rows_ref[at].astype(jnp.float32) * back[at]
        out_ref[at] = out.astype(jnp.bfloat16)
        place = pl.ds(step * (tok // STEPS), tok // STEPS)
        copies.append(pltpu.make_async_copy(out_ref.at[place], out_hbm.at[place], sems.at[step]))
        copies[-1].start()
    for copy in copies:
        copy.wait()


def shards(sizes, hidden, lengths, positive, gain):
    n_dp, n_z, n_y, n_t = sizes
    rows = hidden[0]
    tok, width = rows.shape
    docs = lengths.shape[1]
    count = n_dp * docs
    blocks = n_y * n_t
    lines = docs * width // blocks // LANES
    hbm = pl.BlockSpec(memory_space=pltpu.HBM)
    vmem = pl.BlockSpec(memory_space=pltpu.VMEM)
    params = pltpu.CompilerParams(vmem_limit_bytes=40 * 2**20)

    def array(*dims, dtype=jnp.float32):
        return jax.ShapeDtypeStruct(dims, dtype)

    def summed(parts, copies):
        return pl.pallas_call(
            sum_kernel,
            out_shape=array(copies, lines, LANES),
            in_specs=[vmem],
            out_specs=vmem,
            compiler_params=params,
        )(parts)

    share, member, scale, inverse = pl.pallas_call(
        functools.partial(pool_kernel, sizes),
        out_shape=(array(blocks, lines, LANES), array(tok, LANES), array(tok, LANES), array(count, LANES)),
        in_specs=[hbm, hbm],
        out_specs=(vmem,) * 4,
        scratch_shapes=[
            pltpu.SMEM((n_dp, docs), jnp.int32),
            pltpu.VMEM((tok, width), jnp.bfloat16),
            pltpu.VMEM((tok, LANES), jnp.float32),
            pltpu.SemaphoreType.DMA((CHUNKS + 1,)),
        ],
        compiler_params=params,
    )(pltpu.with_memory_space_constraint(lengths, pltpu.HBM), pltpu.with_memory_space_constraint(rows, pltpu.HBM))
    parts = lax.all_to_all(share, ("y", "t"), 0, 0, tiled=True)
    parts = lax.all_to_all(summed(parts, n_z), "z", 0, 0, tiled=True, axis_index_groups=[list(Z_ORDER)])
    parts = lax.all_to_all(summed(parts, n_dp * n_y), ("dp", "y"), 0, 0, tiled=True)
    sums = lax.all_gather(parts, "t", axis=0)

    grads, loss = pl.pallas_call(
        functools.partial(grad_kernel, sizes),
        out_shape=(array(tok, width, dtype=jnp.bfloat16), array(1, 1)),
        in_specs=[vmem] * 7,
        out_specs=(hbm, vmem),
        scratch_shapes=[
            pltpu.VMEM((count, width), jnp.float32),
            pltpu.VMEM((3 * count, width), jnp.bfloat16),
            pltpu.VMEM((3 * DOC_ROWS, width), jnp.bfloat16),
            pltpu.VMEM((tok, LANES), jnp.bfloat16),
            pltpu.VMEM((tok, width), jnp.bfloat16),
            pltpu.SemaphoreType.DMA((STEPS,)),
        ],
        compiler_params=params,
    )(positive.reshape(1, -1), gain.reshape(1, -1), sums, rows, member, scale, inverse)
    return grads[None], loss.reshape(())


def solution(mesh):
    n_dp, n_seq, n_t = mesh.devices.shape
    n_y = 8 if n_seq % 8 == 0 else 2
    sizes = (n_dp, n_seq // n_y, n_y, n_t)
    inner = Mesh(mesh.devices.reshape(sizes), ("dp", "z", "y", "t"))
    split = P("dp", ("z", "y", "t"), None)
    return jax.shard_map(
        functools.partial(shards, sizes),
        mesh=inner,
        in_specs=(split, P(), P(), P()),
        out_specs=(split, P()),
        check_vma=False,
    )
```

time: 78.6 us -> 74.2 us (0.944)
  local copies, waits for them, and re-layouts: 2.29 us -> 0.02 us
  blocking collectives: 67.2 us -> 65.5 us
    unnamed x12 -> x6, local copies, waits for them, and re-layouts: 2.29 us -> 0.02 us
    all_to_all x1, blocking collectives: 21.9 us -> 19.9 us  [shards(): lax.all_to_all(summed(parts, n_z), 'z', 0, 0, tiled=True, axis_index_grou...]
where the time goes in v2:
time: 74.2 us; the launch traced here: 74 us
  blocking collectives  65.5 us (88%)
  Pallas kernels  7.77 us (10%)
    all_to_all x1, blocking collectives, shards(): parts = lax.all_to_all(share, ('y', 't'), 0, 0, tiled=True)  23.4 us
    all_to_all x1, blocking collectives, shards(): lax.all_to_all(summed(parts, n_z), 'z', 0, 0, tiled=True, axis_index_grou...  19.9 us
    all_to_all x1, blocking collectives, shards(): lax.all_to_all(summed(parts, n_dp * n_y), ('dp', 'y'), 0, 0, tiled=True)  14.5 us
    all_gather x1, blocking collectives, shards(): sums = lax.all_gather(parts, 't', axis=0)  7.75 us
    pallas_call x1, Pallas kernels, shards(): pl.pallas_call(functools.partial(grad_kernel, sizes), out_shape=(array(to...  5 us
    pallas_call x1, Pallas kernels, shards(): pl.pallas_call(functools.partial(pool_kernel, sizes), out_shape=(array(bl...  2.71 us

profile of v2, /device:TPU:1, one launch (start us, length us, event | category | flops | bytes accessed | tf_op | source)
XLA Modules:
  0.0 74.0 jit_solution(7615453602596981577)
XLA Ops:
  0.6 2.7 %shard_map.59 = (f32[16,24,128]{2,1,0:T(8,128)S(1)}, f32[256,128]{1,0:T(8,128)S(1)}, f32[256,128]{1,0:T(8,128)S(1)}, f32[48,128]{1,0:T(8,128)S(1)}) custom-call(s32[4,12]{1,0:T(4,128)} %lens_hbm.1, bf16[256,4096]{1,0:T(8,128)(2,1)} %bitcast.6), custom_call_target="tpu_custom_call" | custom-call | tf_op jit(solution)/shard_map/pallas_call | solution.py:208
  3.3 0.0 copy-start
  3.4 0.0 copy-start.1
  3.4 0.0 copy-start.2
  3.4 23.4 %all_to_all.15.parts_ref = f32[16,24,128]{2,1,0:T(8,128)S(1)} all-to-all(f32[16,24,128]{2,1,0:T(8,128)S(1)} %get-tuple-element.8), channel_id=1, replica_groups=mesh['dp'=4,'z'=12,'y'=8,'t'=2] {'y','t'}, dimensions={0} | all-to-all | bytes 393216 | tf_op jit(solution)/shard_map/all_to_all | solution.py:221
  26.8 19.9 %all_to_all.16.parts_ref = f32[12,24,128]{2,1,0:T(8,128)S(1)} all-to-all(f32[12,24,128]{2,1,0:T(8,128)S(1)} %shard_map.60), channel_id=1, replica_groups={{176,160,144,128,112,96,80,64,48,32,16,0},{177,161,145,129,113,97,81,65..., dimensions={0} | all-to-all | bytes 294912 | tf_op jit(solution)/shard_map/all_to_all | solution.py:222
  46.8 14.5 %all_to_all.17 = f32[32,24,128]{2,1,0:T(8,128)S(1)} all-to-all(f32[32,24,128]{2,1,0:T(8,128)S(1)} %shard_map.61), channel_id=1, replica_groups=mesh['dp'=4,'z'=12,'y'=8,'t'=2] {'dp','y'}, dimensions={0} | all-to-all | bytes 786432 | tf_op jit(solution)/shard_map/all_to_all | solution.py:223
  61.2 7.7 %all-gather = f32[64,24,128]{2,1,0:T(8,128)S(1)} all-gather(f32[32,24,128]{2,1,0:T(8,128)S(1)} %all_to_all.17), channel_id=2, replica_groups=mesh['dp'=4,'z'=12,'y'=8,'t'=2] {'t'}, dimensions={0}, use_global_device_ids=true | all-gather | bytes 1179648 | tf_op jit(solution)/shard_map/all_gather | solution.py:224
  69.0 0.0 copy-done
  69.0 0.0 copy-done.1
  69.0 0.0 copy-done.2
  69.0 5.0 %shard_map.62 = (bf16[256,4096]{1,0:T(8,128)(2,1)}, f32[1,1]{1,0:T(1,128)}) custom-call(s32[1,48]{1,0:T(1,128)S(1)} %bitcast.10, f32[1,4096]{1,0:T(1,128)S(1)} %bitcast.9, f32[2,32,24,128]{3,2,1,0:T(8,128)S(1)} %bitcast.8, bf16[256,4096]{1,0:T(8,128)(2,1)S(1)} %bitcast.7, f32[256,128]{1,0:T(8,128)S(1)} %get-tuple-element.9.member_ref, ...), custom_call_target="tpu_custom_call" | custom-call | tf_op jit(solution)/shard_map/pallas_call | solution.py:226
  (2 shorter events, 0.1 us)
Async XLA Ops:
  3.3 65.6 %copy-start = (bf16[1,256,4096]{2,1,0:T(8,128)(2,1)S(1)}, bf16[1,256,4096]{2,1,0:T(8,128)(2,1)}, u32[]{:S(2)}) copy-start(bf16[1,256,4096]{2,1,0:T(8,128)(2,1)} %param.4) | copy-start | bytes 6291460
  3.4 65.6 %copy-start.1 = (f32[4096]{0:T(1024)S(1)}, f32[4096]{0:T(1024)}, u32[]{:S(2)}) copy-start(f32[4096]{0:T(1024)} %param.7) | copy-start | bytes 49156
  3.4 65.6 %copy-start.2 = (s32[48]{0:T(128)S(1)}, s32[48]{0:T(128)}, u32[]{:S(2)}) copy-start(s32[48]{0:T(128)} %param.6) | copy-start | bytes 580

commit v3 on v2

--- a/solution.py
+++ b/solution.py
@@ -15,14 +15,44 @@
 
 LANES = 128
 DOC_ROWS = 16
-CHUNKS = 8
-STEPS = 4
-Z_ORDER = tuple(range(11, -1, -1))
+WINDOW = 4
+CHUNKS = 4
+STEPS = 8
+MEANS_ORDER = (24, 16, 8, 0, 28, 20, 12, 4, 25, 17, 9, 1, 29, 21, 13, 5, 26, 18, 10, 2, 30, 22, 14, 6, 27, 19, 11, 3, 31, 23, 15, 7)
+Z_ORDER = (11, 5, 10, 4, 9, 3, 8, 2, 7, 1, 6, 0)
 HIGHEST = lax.Precision.HIGHEST
 
 
+def first_doc(lens_ref, group, positions):
+    docs = lens_ref.shape[1]
+    first = jnp.zeros_like(positions)
+    end = jnp.int32(0)
+    for d in range(docs):
+        end = end + lens_ref[group, d]
+        first = first + jnp.where(positions >= end, 1, 0)
+    return first
+
+
+def rounds_needed(lens_ref, tok):
+    groups, docs = lens_ref.shape
+    rounds = jnp.int32(1)
+    for more in range(WINDOW, docs, WINDOW):
+        found = jnp.int32(0)
+        for g in range(groups):
+            starts = [jnp.int32(0)]
+            for d in range(docs):
+                starts.append(starts[-1] + lens_ref[g, d])
+            for d in range(docs - more):
+                shared = lax.div(starts[d + more], tok) <= lax.div(starts[d + 1] - 1, tok)
+                found = jnp.where(shared, 1, found)
+        rounds = rounds + found
+    return rounds
+
+
 def one_hot(lens_ref, group, first, docs, tok):
-    doc = lax.broadcasted_iota(jnp.int32, (1, LANES), 1) % DOC_ROWS
+    lane = lax.broadcasted_iota(jnp.int32, (1, LANES), 1)
+    at_first = first_doc(lens_ref, group, jnp.full((1, LANES), first, jnp.int32))
+    doc = lane % DOC_ROWS + jnp.where(lane >= LANES // 2, at_first, 0)
     starts = jnp.zeros((1, LANES), jnp.int32)
     ends = jnp.zeros((1, LANES), jnp.int32)
     total = jnp.int32(0)
@@ -47,12 +77,13 @@
 
 
 def pool_kernel(
-    sizes, lens_hbm, rows_hbm, out_ref, member_ref, scale_ref, inverse_ref, lens_ref, rows_ref, weights_ref, sems
+    sizes, lens_hbm, rows_hbm, out_ref, more_ref, first_ref, rounds_ref, member_ref, scale_ref, inverse_ref,
+    rows_ref, lens_ref, weights_ref, sems,
 ):
     n_dp, _, n_y, n_t = sizes
     docs = lens_ref.shape[1]
     tok, width = rows_ref.shape
-    blocks = out_ref.shape[0]
+    blocks, part_rows, _ = out_ref.shape
     cut = width // blocks
     lens_copy = pltpu.make_async_copy(lens_hbm, lens_ref, sems.at[CHUNKS])
     lens_copy.start()
@@ -62,8 +93,12 @@
         copies.append(pltpu.make_async_copy(rows_hbm.at[at], rows_ref.at[at], sems.at[chunk]))
         copies[-1].start()
     lens_copy.wait()
-    shard = (lax.axis_index("z") * n_y + lax.axis_index("y")) * n_t + lax.axis_index("t")
-    member_ref[...] = one_hot(lens_ref, lax.axis_index("dp"), shard * tok, docs, tok)
+    group, plane = lax.axis_index("dp"), lax.axis_index("z") * (n_y * n_t)
+    shard = plane + lax.axis_index("y") * n_t + lax.axis_index("t")
+    member_ref[...] = one_hot(lens_ref, group, shard * tok, docs, tok)
+    sender = lax.broadcasted_iota(jnp.int32, first_ref.shape, 1) // part_rows
+    first_ref[...] = first_doc(lens_ref, group, (plane + sender) * tok)
+    rounds_ref[0, 0] = rounds_needed(lens_ref, tok)
     line = lax.broadcasted_iota(jnp.int32, inverse_ref.shape, 0)
     size = jnp.ones(inverse_ref.shape, jnp.float32)
     for g in range(n_dp):
@@ -77,17 +112,37 @@
         scale = lax.rsqrt(jnp.sum(values * values, axis=1, keepdims=True) * (1.0 / width) + norm_eps)
         scale_ref[at] = jnp.broadcast_to(scale, (tok // CHUNKS, LANES))
         weights_ref[at] = member_ref[at] * scale
-    high, low = halves(jnp.transpose(weights_ref[...])[:DOC_ROWS])
+    half = LANES // 2
+    high, low = halves(jnp.transpose(weights_ref[...])[half : half + DOC_ROWS])
     weights = jnp.concatenate([high, low], axis=0)
     for block in range(blocks):
         part = jnp.dot(
             weights, rows_ref[:, block * cut : (block + 1) * cut], preferred_element_type=jnp.float32
         )
-        both = part[:docs] + part[DOC_ROWS : DOC_ROWS + docs]
+        both = part[:DOC_ROWS] + part[DOC_ROWS:]
         for column in range(cut // LANES):
-            out_ref[block, column * docs : (column + 1) * docs, :] = both[
-                :, column * LANES : (column + 1) * LANES
-            ]
+            at, lanes = slice(column * WINDOW, (column + 1) * WINDOW), slice(column * LANES, (column + 1) * LANES)
+            out_ref[block, at] = both[:WINDOW, lanes]
+            for r in range(more_ref.shape[0]):
+                more_ref[r, block, at] = both[(r + 1) * WINDOW : (r + 2) * WINDOW, lanes]
+
+
+def place_kernel(docs, round_ref, first_ref, parts_ref, total_ref, out_ref):
+    senders, part_rows, _ = parts_ref.shape
+    shape = (out_ref.shape[0], senders * part_rows)
+    line = lax.broadcasted_iota(jnp.int32, shape, 0)
+    lane = lax.broadcasted_iota(jnp.int32, shape, 1) % part_rows
+    doc = first_ref[:1, : shape[1]] + lane % WINDOW + round_ref[0, 0] * WINDOW
+    here = (line // docs == lane // WINDOW) & (line % docs == doc)
+    parts = parts_ref[...].reshape(shape[1], LANES)
+    out_ref[...] = total_ref[...] + jnp.dot(
+        jnp.where(here, 1.0, 0.0), parts, precision=HIGHEST, preferred_element_type=jnp.float32
+    )
+
+
+def copy_kernel(total_ref, out_ref):
+    for k in range(out_ref.shape[0]):
+        out_ref[k] = total_ref[...]
 
 
 def sum_kernel(parts_ref, out_ref):
@@ -129,7 +184,7 @@
 
 def grad_kernel(
     sizes, positive_ref, gain_ref, sums_ref, rows_ref, member_ref, scale_ref, inverse_ref,
-    out_hbm, loss_ref, means_ref, parts_ref, grads_ref, weights_ref, out_ref, sems,
+    out_hbm, loss_ref, means_ref, parts_ref, grads_ref, out_ref, sems,
 ):
     n_dp, _, n_y, n_t = sizes
     tok, width = rows_ref.shape
@@ -142,7 +197,7 @@
                 for column in range(columns):
                     start = ((y * n_t + t) * columns + column) * LANES
                     means_ref[g * docs : (g + 1) * docs, start : start + LANES] = sums_ref[
-                        t, g * n_y + y, column * docs : (column + 1) * docs, :
+                        t, MEANS_ORDER.index(g * n_y + y), column * docs : (column + 1) * docs, :
                     ]
     inverse = inverse_ref[...]
     means = means_ref[...] * gain_ref[...] * inverse[:, :1]
@@ -158,22 +213,20 @@
     grads_ref[DOC_ROWS : 2 * DOC_ROWS] = low
     grads_ref[2 * DOC_ROWS :] = high
 
-    member, scale = member_ref[...], scale_ref[...]
-    inner = lax.dot_general(
-        rows_ref[...], grads_ref[: 2 * DOC_ROWS], (((1,), (1,)), ((), ())), preferred_element_type=jnp.float32
-    )
-    inner = jnp.sum(inner * member[:, : 2 * DOC_ROWS], axis=1, keepdims=True)
-    back = scale[:, :1] * scale[:, :1] * scale[:, :1] * inner * (1.0 / width)
-    high, low = halves(member * scale)
-    lane = lax.broadcasted_iota(jnp.int32, member.shape, 1)
-    weights = jnp.where(lane < 2 * DOC_ROWS, high.astype(jnp.float32), low.astype(jnp.float32))
-    weights_ref[...] = weights.astype(jnp.bfloat16)
     copies = []
     for step in range(STEPS):
         at = slice(step * (tok // STEPS), (step + 1) * (tok // STEPS))
-        forward = jnp.dot(weights_ref[at, : 3 * DOC_ROWS], grads_ref[...], preferred_element_type=jnp.float32)
-        out = forward - rows_ref[at].astype(jnp.float32) * back[at]
-        out_ref[at] = out.astype(jnp.bfloat16)
+        member, scale, rows = member_ref[at], scale_ref[at], rows_ref[at]
+        high, low = halves(member * scale)
+        lane = lax.broadcasted_iota(jnp.int32, member.shape, 1)
+        weights = jnp.where(lane < 2 * DOC_ROWS, high.astype(jnp.float32), low.astype(jnp.float32))
+        forward = jnp.dot(
+            weights[:, : 3 * DOC_ROWS].astype(jnp.bfloat16), grads_ref[...], preferred_element_type=jnp.float32
+        )
+        values = rows.astype(jnp.float32)
+        inner = jnp.sum(forward * values, axis=1, keepdims=True)
+        back = scale[:, :1] * scale[:, :1] * inner * (1.0 / width)
+        out_ref[at] = (forward - rows.astype(jnp.float32) * back).astype(jnp.bfloat16)
         place = pl.ds(step * (tok // STEPS), tok // STEPS)
         copies.append(pltpu.make_async_copy(out_ref.at[place], out_hbm.at[place], sems.at[step]))
         copies[-1].start()
@@ -191,6 +244,7 @@
     lines = docs * width // blocks // LANES
     hbm = pl.BlockSpec(memory_space=pltpu.HBM)
     vmem = pl.BlockSpec(memory_space=pltpu.VMEM)
+    smem = pl.BlockSpec(memory_space=pltpu.SMEM)
     params = pltpu.CompilerParams(vmem_limit_bytes=40 * 2**20)
 
     def array(*dims, dtype=jnp.float32):
@@ -205,22 +259,56 @@
             compiler_params=params,
         )(parts)
 
-    share, member, scale, inverse = pl.pallas_call(
+    def placed(r, first, parts, total):
+        return pl.pallas_call(
+            functools.partial(place_kernel, docs),
+            out_shape=array(lines, LANES),
+            in_specs=[smem, vmem, vmem, vmem],
+            out_specs=vmem,
+            compiler_params=params,
+        )(jnp.full((1, 1), r, jnp.int32), first, parts, total)
+
+    share, more, first, rounds, member, scale, inverse, held = pl.pallas_call(
         functools.partial(pool_kernel, sizes),
-        out_shape=(array(blocks, lines, LANES), array(tok, LANES), array(tok, LANES), array(count, LANES)),
+        out_shape=(
+            array(blocks, lines // docs * WINDOW, LANES),
+            array(-(-docs // WINDOW) - 1, blocks, lines // docs * WINDOW, LANES),
+            array(8, LANES, dtype=jnp.int32),
+            array(1, 1, dtype=jnp.int32),
+            array(tok, LANES),
+            array(tok, LANES),
+            array(count, LANES),
+            array(tok, width, dtype=jnp.bfloat16),
+        ),
         in_specs=[hbm, hbm],
-        out_specs=(vmem,) * 4,
+        out_specs=(vmem, vmem, vmem, smem, vmem, vmem, vmem, vmem),
         scratch_shapes=[
             pltpu.SMEM((n_dp, docs), jnp.int32),
-            pltpu.VMEM((tok, width), jnp.bfloat16),
             pltpu.VMEM((tok, LANES), jnp.float32),
             pltpu.SemaphoreType.DMA((CHUNKS + 1,)),
         ],
         compiler_params=params,
     )(pltpu.with_memory_space_constraint(lengths, pltpu.HBM), pltpu.with_memory_space_constraint(rows, pltpu.HBM))
+
+    def exchange(state):
+        r, total = state
+        parts = lax.all_to_all(
+            lax.dynamic_index_in_dim(more, r - 1, 0, keepdims=False), ("y", "t"), 0, 0, tiled=True
+        )
+        return r + 1, placed(r, first, parts, total)
+
     parts = lax.all_to_all(share, ("y", "t"), 0, 0, tiled=True)
-    parts = lax.all_to_all(summed(parts, n_z), "z", 0, 0, tiled=True, axis_index_groups=[list(Z_ORDER)])
-    parts = lax.all_to_all(summed(parts, n_dp * n_y), ("dp", "y"), 0, 0, tiled=True)
+    total = placed(0, first, parts, jnp.zeros((lines, LANES), jnp.float32))
+    _, total = lax.while_loop(lambda state: state[0] < rounds[0, 0], exchange, (jnp.int32(1), total))
+    copies = pl.pallas_call(
+        copy_kernel,
+        out_shape=array(n_z, lines, LANES),
+        in_specs=[vmem],
+        out_specs=vmem,
+        compiler_params=params,
+    )(total)
+    parts = lax.all_to_all(copies, "z", 0, 0, tiled=True, axis_index_groups=[list(Z_ORDER)])
+    parts = lax.all_to_all(summed(parts, n_dp * n_y), ("dp", "y"), 0, 0, tiled=True, axis_index_groups=[list(MEANS_ORDER)])
     sums = lax.all_gather(parts, "t", axis=0)
 
     grads, loss = pl.pallas_call(
@@ -232,12 +320,11 @@
             pltpu.VMEM((count, width), jnp.float32),
             pltpu.VMEM((3 * count, width), jnp.bfloat16),
             pltpu.VMEM((3 * DOC_ROWS, width), jnp.bfloat16),
-            pltpu.VMEM((tok, LANES), jnp.bfloat16),
             pltpu.VMEM((tok, width), jnp.bfloat16),
             pltpu.SemaphoreType.DMA((STEPS,)),
         ],
         compiler_params=params,
-    )(positive.reshape(1, -1), gain.reshape(1, -1), sums, rows, member, scale, inverse)
+    )(positive.reshape(1, -1), gain.reshape(1, -1), sums, held, member, scale, inverse)
     return grads[None], loss.reshape(())
 
 

time: 74.2 us -> 70.4 us (0.949)
  blocking collectives: 65.5 us -> 38.8 us
  starting transfers between devices: 0 us -> 13.8 us
  waiting for transfers between devices: 0 us -> 7.84 us
    all_to_all x3 -> x2, blocking collectives: 57.8 us -> 31.8 us  [the longest x1 17.3 us: shards(): lax.all_to_all(copies, 'z', 0, 0, tiled=True, axis_index_groups=[list(Z_O...]
    all_to_all x0 -> x1, starting transfers between devices: none -> 13.8 us  [shards(): parts = lax.all_to_all(share, ('y', 't'), 0, 0, tiled=True)]
    all_to_all x0 -> x1, waiting for transfers between devices: none -> 7.84 us  [shards(): parts = lax.all_to_all(share, ('y', 't'), 0, 0, tiled=True)]
    all_gather x1, blocking collectives: 7.75 us -> 6.99 us  [shards(): sums = lax.all_gather(parts, 't', axis=0)]
  transfers between devices with their start and end apart: 0 -> 1, of which waited for: 0 -> 1; matrix products, arithmetic and copies ran while one was open for 0% -> 0% of each run, Pallas kernels for 0% -> 0%
where the time goes in v3:
time: 70.4 us; the launch traced here: 69.6 us
  blocking collectives  38.8 us (55%)
  starting transfers between devices  13.8 us (20%)
  waiting for transfers between devices  7.84 us (11%)
  Pallas kernels  7.8 us (11%)
    all_to_all x1, blocking collectives, shards(): lax.all_to_all(copies, 'z', 0, 0, tiled=True, axis_index_groups=[list(Z_O...  17.3 us
    all_to_all x1, blocking collectives, shards(): lax.all_to_all(summed(parts, n_dp * n_y), ('dp', 'y'), 0, 0, tiled=True,...  14.5 us
    all_to_all x1, starting transfers between devices, shards(): parts = lax.all_to_all(share, ('y', 't'), 0, 0, tiled=True)  13.8 us
    all_to_all x1, waiting for transfers between devices, shards(): parts = lax.all_to_all(share, ('y', 't'), 0, 0, tiled=True)  7.84 us
    all_gather x1, blocking collectives, shards(): sums = lax.all_gather(parts, 't', axis=0)  6.99 us
    pallas_call x1, Pallas kernels, shards(): pl.pallas_call(functools.partial(grad_kernel, sizes), out_shape=(array(to...  4.57 us
    pallas_call x1, Pallas kernels, shards(): pl.pallas_call(functools.partial(pool_kernel, sizes), out_shape=(array(bl...  3.01 us
  transfers between devices with their start and end apart: 1, of which 1 were waited for; matrix products, arithmetic and copies ran while one was open for 0% of the time, Pallas kernels for 0%

profile of v3, /device:TPU:1, one launch (start us, length us, event | category | flops | bytes accessed | tf_op | source)
XLA Modules:
  0.0 69.6 jit_solution(1191536246852979090)
XLA Ops:
  0.6 3.0 %shard_map.59 = (f32[16,8,128]{2,1,0:T(8,128)}, f32[2,16,8,128]{3,2,1,0:T(8,128)S(1)}, s32[8,128]{1,0:T(8,128)S(1)}, s32[1,1]{1,0:T(1,128)}, f32[256,128]{1,0:T(...) custom-call(s32[4,12]{1,0:T(4,128)} %lens_hbm.1, bf16[256,4096]{1,0:T(8,128)(2,1)} %bitcast.18), custom_call_target="tpu_custom_call" | custom-call | tf_op jit(solution)/shard_map/pallas_call | solution.py:271
  3.7 13.8 %all-to-all-start.1 = ((f32[16,8,128]{2,1,0:T(8,128)}), f32[16,8,128]{2,1,0:T(8,128)S(1)}, u32[]{:S(2)}, u32[]{:S(2)}) async-start(f32[16,8,128]{2,1,0:T(8,128)} %get-tuple-element.118), calls=%async_computation.1 | async-start | bytes 131072 | tf_op jit(solution)/shard_map/all_to_all | solution.py:300
  17.5 7.8 %all-to-all-done.1.parts_ref = f32[16,8,128]{2,1,0:T(8,128)S(1)} async-done(((f32[16,8,128]{2,1,0:T(8,128)}), f32[16,8,128]{2,1,0:T(8,128)S(1)}, u32[]{:S(2)}, u32[]{:S(2)}) %all-to-all-start.1) | async-done | bytes 65568 | tf_op jit(solution)/shard_map/all_to_all | solution.py:300
  25.3 0.2 shard_map.60
  25.5 0.0 copy-start
  25.5 0.0 copy-start.1
  25.5 0.7 %while.14 = (s32[]{:T(128)}, f32[24,128]{1,0:T(8,128)S(1)}, s32[1,1]{1,0:T(1,128)}, f32[2,16,8,128]{3,2,1,0:T(8,128)S(1)}, s32[8,128]{1,0:T(8,128)S(1)}, /*index=5*/s32[]{:T(128)}, s32[]{:T(128)}, s32[]{:T(128)}) while((s32[]{:T(128)}, f32[24,128]{1,0:T(8,128)S(1)}, s32[1,1]{1,0:T(1,128)}, f32[2,16,8,128]{3,2,1,0:T(8,128)S(1)}, ...), condition=%wide.region_1.2_spmd, body=%wide.region_0.1_spmd.sunk | while | flops 5 | bytes 352419 | solution.py:302
  26.2 17.3 %all_to_all.21.parts_ref = f32[12,24,128]{2,1,0:T(8,128)S(1)} all-to-all(f32[12,24,128]{2,1,0:T(8,128)S(1)} %shard_map.61), channel_id=1, replica_groups={{176,80,160,64,144,48,128,32,112,16,96,0},{177,81,161,65,145,49,129,33,..., dimensions={0} | all-to-all | bytes 294912 | tf_op jit(solution)/shard_map/all_to_all | solution.py:310
  43.5 14.5 %all_to_all.22 = f32[32,24,128]{2,1,0:T(8,128)S(1)} all-to-all(f32[32,24,128]{2,1,0:T(8,128)S(1)} %shard_map.62), channel_id=1, replica_groups={{576,384,192,0,584,392,200,8,578,386,194,2,586,394,202,10,580,388,196,4..., dimensions={0} | all-to-all | bytes 786432 | tf_op jit(solution)/shard_map/all_to_all | solution.py:311
  58.1 7.0 %all-gather = f32[64,24,128]{2,1,0:T(8,128)S(1)} all-gather(f32[32,24,128]{2,1,0:T(8,128)S(1)} %all_to_all.22), channel_id=2, replica_groups=mesh['dp'=4,'z'=12,'y'=8,'t'=2] {'t'}, dimensions={0}, use_global_device_ids=true | all-gather | bytes 1179648 | tf_op jit(solution)/shard_map/all_gather | solution.py:312
  65.1 0.0 copy-done
  65.1 0.0 copy-done.1
  65.1 4.6 %shard_map.63 = (bf16[256,4096]{1,0:T(8,128)(2,1)}, f32[1,1]{1,0:T(1,128)}) custom-call(s32[1,48]{1,0:T(1,128)S(1)} %bitcast.17, f32[1,4096]{1,0:T(1,128)S(1)} %bitcast.16, f32[2,32,24,128]{3,2,1,0:T(8,128)S(1)} %bitcast.15, bf16[256,4096]{1,0:T(8,128)(2,1)S(1)} %get-tuple-element.122.rows_ref, f32[256,128]{1,0:T(8,128)S(1)} %get-tuple-element.123.member_ref, ...), custom_call_target="tpu_custom_call" | custom-call | tf_op jit(solution)/shard_map/pallas_call | solution.py:314
  (3 shorter events, 0.1 us)
Async XLA Ops:
  3.7 21.7 %all-to-all-start.1 = ((f32[16,8,128]{2,1,0:T(8,128)}), f32[16,8,128]{2,1,0:T(8,128)S(1)}, u32[]{:S(2)}, u32[]{:S(2)}) async-start(f32[16,8,128]{2,1,0:T(8,128)} %get-tuple-element.118), calls=%async_computation.1 | async-start | bytes 131072 | tf_op jit(solution)/shard_map/all_to_all | solution.py:300
  25.5 39.6 %copy-start = (f32[4096]{0:T(1024)S(1)}, f32[4096]{0:T(1024)}, u32[]{:S(2)}) copy-start(f32[4096]{0:T(1024)} %param.9) | copy-start | bytes 49156
  25.5 39.6 %copy-start.1 = (s32[48]{0:T(128)S(1)}, s32[48]{0:T(128)}, u32[]{:S(2)}) copy-start(s32[48]{0:T(128)} %param.8) | copy-start | bytes 580

commit v4 on v3

--- a/solution.py
+++ b/solution.py
@@ -129,20 +129,17 @@
 
 def place_kernel(docs, round_ref, first_ref, parts_ref, total_ref, out_ref):
     senders, part_rows, _ = parts_ref.shape
-    shape = (out_ref.shape[0], senders * part_rows)
+    shape = (out_ref.shape[1], senders * part_rows)
     line = lax.broadcasted_iota(jnp.int32, shape, 0)
     lane = lax.broadcasted_iota(jnp.int32, shape, 1) % part_rows
     doc = first_ref[:1, : shape[1]] + lane % WINDOW + round_ref[0, 0] * WINDOW
     here = (line // docs == lane // WINDOW) & (line % docs == doc)
     parts = parts_ref[...].reshape(shape[1], LANES)
-    out_ref[...] = total_ref[...] + jnp.dot(
+    total = total_ref[...] + jnp.dot(
         jnp.where(here, 1.0, 0.0), parts, precision=HIGHEST, preferred_element_type=jnp.float32
     )
-
-
-def copy_kernel(total_ref, out_ref):
     for k in range(out_ref.shape[0]):
-        out_ref[k] = total_ref[...]
+        out_ref[k] = total
 
 
 def sum_kernel(parts_ref, out_ref):
@@ -259,10 +256,10 @@
             compiler_params=params,
         )(parts)
 
-    def placed(r, first, parts, total):
+    def placed(r, first, parts, total, copies):
         return pl.pallas_call(
             functools.partial(place_kernel, docs),
-            out_shape=array(lines, LANES),
+            out_shape=array(copies, lines, LANES),
             in_specs=[smem, vmem, vmem, vmem],
             out_specs=vmem,
             compiler_params=params,
@@ -295,18 +292,13 @@
         parts = lax.all_to_all(
             lax.dynamic_index_in_dim(more, r - 1, 0, keepdims=False), ("y", "t"), 0, 0, tiled=True
         )
-        return r + 1, placed(r, first, parts, total)
-
+        return r + 1, placed(r, first, parts, total, 1)[0]
+
+    _, rest = lax.while_loop(
+        lambda state: state[0] < rounds[0, 0], exchange, (jnp.int32(1), jnp.zeros((lines, LANES), jnp.float32))
+    )
     parts = lax.all_to_all(share, ("y", "t"), 0, 0, tiled=True)
-    total = placed(0, first, parts, jnp.zeros((lines, LANES), jnp.float32))
-    _, total = lax.while_loop(lambda state: state[0] < rounds[0, 0], exchange, (jnp.int32(1), total))
-    copies = pl.pallas_call(
-        copy_kernel,
-        out_shape=array(n_z, lines, LANES),
-        in_specs=[vmem],
-        out_specs=vmem,
-        compiler_params=params,
-    )(total)
+    copies = placed(0, first, parts, rest, n_z)
     parts = lax.all_to_all(copies, "z", 0, 0, tiled=True, axis_index_groups=[list(Z_ORDER)])
     parts = lax.all_to_all(summed(parts, n_dp * n_y), ("dp", "y"), 0, 0, tiled=True, axis_index_groups=[list(MEANS_ORDER)])
     sums = lax.all_gather(parts, "t", axis=0)

time: 70.4 us -> 69.5 us (0.987)
  blocking collectives: 38.8 us -> 60.2 us
  starting transfers between devices: 13.8 us -> 0 us
  waiting for transfers between devices: 7.84 us -> 0 us
    all_to_all x0 -> x1, blocking collectives: none -> 20.8 us  [shards(): parts = lax.all_to_all(share, ('y', 't'), 0, 0, tiled=True)]
    all_to_all x1 -> x0, starting transfers between devices: 13.8 us -> none  [shards(): parts = lax.all_to_all(share, ('y', 't'), 0, 0, tiled=True)]
    all_to_all x1 -> x0, waiting for transfers between devices: 7.84 us -> none  [shards(): parts = lax.all_to_all(share, ('y', 't'), 0, 0, tiled=True)]
  transfers between devices with their start and end apart: 1 -> 0, of which waited for: 1 -> 0; matrix products, arithmetic and copies ran while one was open for 0% -> 0% of each run, Pallas kernels for 0% -> 0%
where the time goes in v4:
time: 69.5 us; the launch traced here: 68.8 us
  blocking collectives  60.2 us (87%)
  Pallas kernels  7.17 us (10%)
  loops' own time  0.7 us (1%)
    all_to_all x1, blocking collectives, shards(): parts = lax.all_to_all(share, ('y', 't'), 0, 0, tiled=True)  20.8 us
    all_to_all x1, blocking collectives, shards(): lax.all_to_all(copies, 'z', 0, 0, tiled=True, axis_index_groups=[list(Z_O...  17.9 us
    all_to_all x1, blocking collectives, shards(): lax.all_to_all(summed(parts, n_dp * n_y), ('dp', 'y'), 0, 0, tiled=True,...  14.5 us
    all_gather x1, blocking collectives, shards(): sums = lax.all_gather(parts, 't', axis=0)  6.99 us
    pallas_call x1, Pallas kernels, shards(): pl.pallas_call(functools.partial(grad_kernel, sizes), out_shape=(array(to...  4.56 us
    pallas_call x1, Pallas kernels, shards(): pl.pallas_call(functools.partial(pool_kernel, sizes), out_shape=(array(bl...  2.39 us

profile of v4, /device:TPU:1, one launch (start us, length us, event | category | flops | bytes accessed | tf_op | source)
XLA Modules:
  0.0 68.8 jit_solution(15621344250268957867)
XLA Ops:
  0.6 2.4 %shard_map.59 = (f32[16,8,128]{2,1,0:T(8,128)S(1)}, f32[2,16,8,128]{3,2,1,0:T(8,128)S(1)}, s32[8,128]{1,0:T(8,128)S(1)}, s32[1,1]{1,0:T(1,128)}, f32[256,128]{1,...) custom-call(s32[4,12]{1,0:T(4,128)} %lens_hbm.1, ...), custom_call_target="tpu_custom_call" | custom-call | tf_op jit(solution)/shard_map/pallas_call | solution.py:268
  3.0 0.7 %while.14 = (s32[]{:T(128)}, f32[24,128]{1,0:T(8,128)S(1)}, s32[1,1]{1,0:T(1,128)}, f32[2,16,8,128]{3,2,1,0:T(8,128)S(1)}, s32[8,128]{1,0:T(8,128)S(1)}, /*index=5*/s32[]{:T(128)}, s32[]{:T(128)}, s32[]{:T(128)}) while((s32[]{:T(128)}, f32[24,128]{1,0:T(8,128)S(1)}, s32[1,1]{1,0:T(1,128)}, f32[2,16,8,128]{3,2,1,0:T(8,128)S(1)}, ...), condition=%wide.region_1.2_spmd, body=%wide.region_0.1_spmd.sunk | while | flops 5 | bytes 352419 | solution.py:297
  3.7 0.0 copy-start
  3.8 0.0 copy-start.1
  3.8 20.8 %all_to_all.21.parts_ref = f32[16,8,128]{2,1,0:T(8,128)S(1)} all-to-all(f32[16,8,128]{2,1,0:T(8,128)S(1)} %get-tuple-element.118), channel_id=1, replica_groups=mesh['dp'=4,'z'=12,'y'=8,'t'=2] {'y','t'}, dimensions={0} | all-to-all | bytes 131072 | tf_op jit(solution)/shard_map/all_to_all | solution.py:300
  24.5 0.2 shard_map.60
  24.7 17.9 %all_to_all.22.parts_ref = f32[12,24,128]{2,1,0:T(8,128)S(1)} all-to-all(f32[12,24,128]{2,1,0:T(8,128)S(1)} %shard_map.60), channel_id=1, replica_groups={{176,80,160,64,144,48,128,32,112,16,96,0},{177,81,161,65,145,49,129,33,..., dimensions={0} | all-to-all | bytes 294912 | tf_op jit(solution)/shard_map/all_to_all | solution.py:302
  42.7 14.5 %all_to_all.23 = f32[32,24,128]{2,1,0:T(8,128)S(1)} all-to-all(f32[32,24,128]{2,1,0:T(8,128)S(1)} %shard_map.61), channel_id=1, replica_groups={{576,384,192,0,584,392,200,8,578,386,194,2,586,394,202,10,580,388,196,4..., dimensions={0} | all-to-all | bytes 786432 | tf_op jit(solution)/shard_map/all_to_all | solution.py:303
  57.2 7.0 %all-gather = f32[64,24,128]{2,1,0:T(8,128)S(1)} all-gather(f32[32,24,128]{2,1,0:T(8,128)S(1)} %all_to_all.23), channel_id=2, replica_groups=mesh['dp'=4,'z'=12,'y'=8,'t'=2] {'t'}, dimensions={0}, use_global_device_ids=true | all-gather | bytes 1179648 | tf_op jit(solution)/shard_map/all_gather | solution.py:304
  64.2 0.0 copy-done
  64.2 0.0 copy-done.1
  64.2 4.6 %shard_map.62 = (bf16[256,4096]{1,0:T(8,128)(2,1)}, f32[1,1]{1,0:T(1,128)}) custom-call(s32[1,48]{1,0:T(1,128)S(1)} %bitcast.20, f32[1,4096]{1,0:T(1,128)S(1)} %bitcast.19, f32[2,32,24,128]{3,2,1,0:T(8,128)S(1)} %bitcast.18, bf16[256,4096]{1,0:T(8,128)(2,1)S(1)} %get-tuple-element.122.rows_ref, f32[256,128]{1,0:T(8,128)S(1)} %get-tuple-element.123.member_ref, ...), custom_call_target="tpu_custom_call" | custom-call | tf_op jit(solution)/shard_map/pallas_call | solution.py:306
  (2 shorter events, 0.0 us)
Async XLA Ops:
  3.7 60.5 %copy-start = (f32[4096]{0:T(1024)S(1)}, f32[4096]{0:T(1024)}, u32[]{:S(2)}) copy-start(f32[4096]{0:T(1024)} %param.9) | copy-start | bytes 49156
  3.8 60.5 %copy-start.1 = (s32[48]{0:T(128)S(1)}, s32[48]{0:T(128)}, u32[]{:S(2)}) copy-start(s32[48]{0:T(128)} %param.8) | copy-start | bytes 580

commit v5 on v4

--- a/solution.py
+++ b/solution.py
@@ -77,8 +77,8 @@
 
 
 def pool_kernel(
-    sizes, lens_hbm, rows_hbm, out_ref, more_ref, first_ref, rounds_ref, member_ref, scale_ref, inverse_ref,
-    rows_ref, lens_ref, weights_ref, sems,
+    sizes, lens_hbm, rows_hbm, out_ref, more_ref, first_ref, rounds_ref, forward_ref, scale_ref, inverse_ref,
+    rows_ref, lens_ref, member_ref, weights_ref, sems,
 ):
     n_dp, _, n_y, n_t = sizes
     docs = lens_ref.shape[1]
@@ -111,7 +111,12 @@
         values = rows_ref[at].astype(jnp.float32)
         scale = lax.rsqrt(jnp.sum(values * values, axis=1, keepdims=True) * (1.0 / width) + norm_eps)
         scale_ref[at] = jnp.broadcast_to(scale, (tok // CHUNKS, LANES))
-        weights_ref[at] = member_ref[at] * scale
+        weights = member_ref[at] * scale
+        weights_ref[at] = weights
+        high, low = halves(weights)
+        lane = lax.broadcasted_iota(jnp.int32, weights.shape, 1)
+        forward = jnp.where(lane < 2 * DOC_ROWS, high.astype(jnp.float32), low.astype(jnp.float32))
+        forward_ref[at] = forward.astype(jnp.bfloat16)
     half = LANES // 2
     high, low = halves(jnp.transpose(weights_ref[...])[half : half + DOC_ROWS])
     weights = jnp.concatenate([high, low], axis=0)
@@ -180,7 +185,7 @@
 
 
 def grad_kernel(
-    sizes, positive_ref, gain_ref, sums_ref, rows_ref, member_ref, scale_ref, inverse_ref,
+    sizes, positive_ref, gain_ref, sums_ref, rows_ref, forward_ref, scale_ref, inverse_ref,
     out_hbm, loss_ref, means_ref, parts_ref, grads_ref, out_ref, sems,
 ):
     n_dp, _, n_y, n_t = sizes
@@ -213,12 +218,9 @@
     copies = []
     for step in range(STEPS):
         at = slice(step * (tok // STEPS), (step + 1) * (tok // STEPS))
-        member, scale, rows = member_ref[at], scale_ref[at], rows_ref[at]
-        high, low = halves(member * scale)
-        lane = lax.broadcasted_iota(jnp.int32, member.shape, 1)
-        weights = jnp.where(lane < 2 * DOC_ROWS, high.astype(jnp.float32), low.astype(jnp.float32))
+        scale, rows = scale_ref[at], rows_ref[at]
         forward = jnp.dot(
-            weights[:, : 3 * DOC_ROWS].astype(jnp.bfloat16), grads_ref[...], preferred_element_type=jnp.float32
+            forward_ref[at, : 3 * DOC_ROWS], grads_ref[...], preferred_element_type=jnp.float32
         )
         values = rows.astype(jnp.float32)
         inner = jnp.sum(forward * values, axis=1, keepdims=True)
@@ -265,14 +267,14 @@
             compiler_params=params,
         )(jnp.full((1, 1), r, jnp.int32), first, parts, total)
 
-    share, more, first, rounds, member, scale, inverse, held = pl.pallas_call(
+    share, more, first, rounds, forward, scale, inverse, held = pl.pallas_call(
         functools.partial(pool_kernel, sizes),
         out_shape=(
             array(blocks, lines // docs * WINDOW, LANES),
             array(-(-docs // WINDOW) - 1, blocks, lines // docs * WINDOW, LANES),
             array(8, LANES, dtype=jnp.int32),
             array(1, 1, dtype=jnp.int32),
-            array(tok, LANES),
+            array(tok, LANES, dtype=jnp.bfloat16),
             array(tok, LANES),
             array(count, LANES),
             array(tok, width, dtype=jnp.bfloat16),
@@ -281,6 +283,7 @@
         out_specs=(vmem, vmem, vmem, smem, vmem, vmem, vmem, vmem),
         scratch_shapes=[
             pltpu.SMEM((n_dp, docs), jnp.int32),
+            pltpu.VMEM((tok, LANES), jnp.float32),
             pltpu.VMEM((tok, LANES), jnp.float32),
             pltpu.SemaphoreType.DMA((CHUNKS + 1,)),
         ],
@@ -316,7 +319,7 @@
             pltpu.SemaphoreType.DMA((STEPS,)),
         ],
         compiler_params=params,
-    )(positive.reshape(1, -1), gain.reshape(1, -1), sums, held, member, scale, inverse)
+    )(positive.reshape(1, -1), gain.reshape(1, -1), sums, held, forward, scale, inverse)
     return grads[None], loss.reshape(())
 
 

time: 69.5 us -> 69.6 us (level)
  no operation moved by 1% of the time
where the time goes in v5:
time: 69.6 us; the launch traced here: 68.8 us
  blocking collectives  60.2 us (86%)
  Pallas kernels  7.2 us (10%)
  loops' own time  0.7 us (1%)
    all_to_all x1, blocking collectives, shards(): parts = lax.all_to_all(share, ('y', 't'), 0, 0, tiled=True)  20.8 us
    all_to_all x1, blocking collectives, shards(): lax.all_to_all(copies, 'z', 0, 0, tiled=True, axis_index_groups=[list(Z_O...  17.9 us
    all_to_all x1, blocking collectives, shards(): lax.all_to_all(summed(parts, n_dp * n_y), ('dp', 'y'), 0, 0, tiled=True,...  14.5 us
    all_gather x1, blocking collectives, shards(): sums = lax.all_gather(parts, 't', axis=0)  6.99 us
    pallas_call x1, Pallas kernels, shards(): pl.pallas_call(functools.partial(grad_kernel, sizes), out_shape=(array(to...  4.57 us
    pallas_call x1, Pallas kernels, shards(): pl.pallas_call(functools.partial(pool_kernel, sizes), out_shape=(array(bl...  2.41 us

profile of v5, /device:TPU:1, one launch (start us, length us, event | category | flops | bytes accessed | tf_op | source)
XLA Modules:
  0.0 68.8 jit_solution(18221067128782388707)
XLA Ops:
  0.6 2.4 %shard_map.59 = (f32[16,8,128]{2,1,0:T(8,128)S(1)}, f32[2,16,8,128]{3,2,1,0:T(8,128)S(1)}, s32[8,128]{1,0:T(8,128)S(1)}, s32[1,1]{1,0:T(1,128)}, bf16[256,128]{1...) custom-call(s32[4,12]{1,0:T(4,128)} %lens_hbm.1, ...), custom_call_target="tpu_custom_call" | custom-call | tf_op jit(solution)/shard_map/pallas_call | solution.py:270
  3.1 0.7 %while.14 = (s32[]{:T(128)}, f32[24,128]{1,0:T(8,128)S(1)}, s32[1,1]{1,0:T(1,128)}, f32[2,16,8,128]{3,2,1,0:T(8,128)S(1)}, s32[8,128]{1,0:T(8,128)S(1)}, /*index=5*/s32[]{:T(128)}, s32[]{:T(128)}, s32[]{:T(128)}) while((s32[]{:T(128)}, f32[24,128]{1,0:T(8,128)S(1)}, s32[1,1]{1,0:T(1,128)}, f32[2,16,8,128]{3,2,1,0:T(8,128)S(1)}, ...), condition=%wide.region_1.2_spmd, body=%wide.region_0.1_spmd.sunk | while | flops 5 | bytes 352419 | solution.py:300
  3.8 0.0 copy-start
  3.8 0.0 copy-start.1
  3.8 20.8 %all_to_all.21.parts_ref = f32[16,8,128]{2,1,0:T(8,128)S(1)} all-to-all(f32[16,8,128]{2,1,0:T(8,128)S(1)} %get-tuple-element.118), channel_id=1, replica_groups=mesh['dp'=4,'z'=12,'y'=8,'t'=2] {'y','t'}, dimensions={0} | all-to-all | bytes 131072 | tf_op jit(solution)/shard_map/all_to_all | solution.py:303
  24.5 0.2 shard_map.60
  24.7 17.9 %all_to_all.22.parts_ref = f32[12,24,128]{2,1,0:T(8,128)S(1)} all-to-all(f32[12,24,128]{2,1,0:T(8,128)S(1)} %shard_map.60), channel_id=1, replica_groups={{176,80,160,64,144,48,128,32,112,16,96,0},{177,81,161,65,145,49,129,33,..., dimensions={0} | all-to-all | bytes 294912 | tf_op jit(solution)/shard_map/all_to_all | solution.py:305
  42.7 14.5 %all_to_all.23 = f32[32,24,128]{2,1,0:T(8,128)S(1)} all-to-all(f32[32,24,128]{2,1,0:T(8,128)S(1)} %shard_map.61), channel_id=1, replica_groups={{576,384,192,0,584,392,200,8,578,386,194,2,586,394,202,10,580,388,196,4..., dimensions={0} | all-to-all | bytes 786432 | tf_op jit(solution)/shard_map/all_to_all | solution.py:306
  57.3 7.0 %all-gather = f32[64,24,128]{2,1,0:T(8,128)S(1)} all-gather(f32[32,24,128]{2,1,0:T(8,128)S(1)} %all_to_all.23), channel_id=2, replica_groups=mesh['dp'=4,'z'=12,'y'=8,'t'=2] {'t'}, dimensions={0}, use_global_device_ids=true | all-gather | bytes 1179648 | tf_op jit(solution)/shard_map/all_gather | solution.py:307
  64.2 0.0 copy-done
  64.2 0.0 copy-done.1
  64.2 4.6 %shard_map.62 = (bf16[256,4096]{1,0:T(8,128)(2,1)}, f32[1,1]{1,0:T(1,128)}) custom-call(s32[1,48]{1,0:T(1,128)S(1)} %bitcast.20, f32[1,4096]{1,0:T(1,128)S(1)} %bitcast.19, f32[2,32,24,128]{3,2,1,0:T(8,128)S(1)} %bitcast.18, bf16[256,4096]{1,0:T(8,128)(2,1)S(1)} %get-tuple-element.122.rows_ref, bf16[256,128]{1,0:T(8,128)(2,1)S(1)} %get-tuple-element.123.forward_ref, ...), custom_call_target="tpu_custom_call" | custom-call | tf_op jit(solution)/shard_map/pallas_call | solution.py:309
  (2 shorter events, 0.0 us)
Async XLA Ops:
  3.8 60.5 %copy-start = (f32[4096]{0:T(1024)S(1)}, f32[4096]{0:T(1024)}, u32[]{:S(2)}) copy-start(f32[4096]{0:T(1024)} %param.9) | copy-start | bytes 49156
  3.8 60.5 %copy-start.1 = (s32[48]{0:T(128)S(1)}, s32[48]{0:T(128)}, u32[]{:S(2)}) copy-start(s32[48]{0:T(128)} %param.8) | copy-start | bytes 580
